TPU v7x, 32 devices: a whole 2x2x4 slice. The times are simulated.
32 devices in a mesh: req: 8 (over y, x, core), tp: 4 (over z).
Axes of the slice: x: 2, y: 2, z: 4, core: 2. Of those that a mesh axis runs over, the one named last changes fastest.
Arguments:
- embeds: bfloat16 [2048, 2048], P(('req', 'tp')), may hold values from -25 to 25
- input_norm_gain: float32 [2048], replicated, may hold values from 0.25 to 1.75
- input_norm_bias: float32 [2048], replicated, may hold values from -3 to 3
- joined_projection_weight: bfloat16 [2048, 6144], P(None, 'tp'), may hold values from -0.125 to 0.125
- joined_projection_bias: float32 [6144], P('tp'), may hold values from -3 to 3
- adapter_down_weight: bfloat16 [4, 2048, 16], replicated, may hold values from -0.125 to 0.125
- adapter_up_weight: bfloat16 [4, 16, 6144], P(None, None, 'tp'), may hold values from -1.5 to 1.5
- attention_out_weight: bfloat16 [2048, 2048], P('tp'), may hold values from -0.125 to 0.125
- attention_out_bias: float32 [2048], replicated, may hold values from -3 to 3
- post_attention_norm_gain: float32 [2048], replicated, may hold values from 0.4 to 1.6
- post_attention_norm_bias: float32 [2048], replicated, may hold values from -3 to 3
- feedforward_up_weight: bfloat16 [2048, 4096], P(None, 'tp'), may hold values from -0.125 to 0.125
- feedforward_up_bias: float32 [4096], P('tp'), may hold values from -3 to 3
- feedforward_down_weight: bfloat16 [4096, 2048], P('tp'), may hold values from -0.09375 to 0.09375
- feedforward_down_bias: float32 [2048], replicated, may hold values from -3 to 3
- stored_keys: bfloat16 [8, 1024, 2048], P('req', None, 'tp'), may hold values from -400 to 400
- stored_values: bfloat16 [8, 1024, 2048], P('req', None, 'tp'), may hold values from -6 to 6
- stored_length: int32 [8], P('req'), may hold values from 2 to 1024, as said below
- tenant_first_request: int32 [3], replicated, may hold values from 1 to 7, as said below
- accept: int32 [2048], P(('req', 'tp')), may hold values 0 or 1
- replacement_token_index: int32 [2048], P('req'), may hold values from 0 to 50175, as said below
- word_embedding_table: bfloat16 [50176, 2048], P('req', 'tp'), may hold values from -6 to 6
Outputs:
- denoised: bfloat16 [2048, 2048], P(('req', 'tp'))
Inputs may be any that keep to these rules, and one draw needn't show every extreme that they name: `stored_length`: one request has exactly 1024 cached positions. `tenant_first_request`: strictly increasing. `replacement_token_index`: of the 256 ids of one index of req, at most 96 lie in the rows o * 6272 to (o + 1) * 6272 - 1 of any one index o of req; one index o receives exactly 96 from every index of req, and every other index receives about equally many.
All inputs are finite; a program needn't handle non-finite values. No bound on the sum of `accept` on one device may be relied on, other than what follows from the above.
Results may differ from a plain program's by a relative error of at most 0.04.
Values may be sent and summed in bfloat16 or wider, within the bound.
A program may use at most 128 MiB of HBM per device.

v0:
```python
import jax
import jax.numpy as jnp
from jax import lax
from jax.sharding import PartitionSpec as P

H = 16
HD = 128
BLK = 256
EPSILON = 1e-05


def layer_norm(residual_state, gain, shift):
    values = residual_state.astype(jnp.float32)
    row_mean = jnp.mean(values, axis=-1, keepdims=True)
    centered = values - row_mean
    variance = jnp.mean(centered * centered, axis=-1, keepdims=True)
    return (centered * lax.rsqrt(variance + EPSILON) * gain + shift).astype(jnp.bfloat16)


def attend(queries, keys_block, values_block, keys_cache, values_cache, length, slopes):
    block_len = queries.shape[0]
    local_heads = queries.shape[1]
    head_size = queries.shape[2]
    score_scale = 1.0 / jnp.sqrt(jnp.float32(head_size))
    block_pos = jnp.arange(block_len)
    query_pos = length + block_pos
    scores = (
        jnp.einsum("qhd,khd->hqk", queries, keys_block, preferred_element_type=jnp.float32)
        * score_scale
    )
    distance = jnp.abs(block_pos[:, None] - block_pos[None, :]).astype(jnp.float32)
    scores = scores - slopes[:, None, None] * distance[None, :, :]
    row_max = jnp.max(scores, axis=-1)
    weights = jnp.exp(scores - row_max[..., None])
    row_total = jnp.sum(weights, axis=-1)
    accum = jnp.einsum(
        "hqk,khd->hqd",
        weights.astype(jnp.bfloat16),
        values_block,
        preferred_element_type=jnp.float32,
    )
    cache_rows = keys_cache.shape[0]
    tile_len = min(512, cache_rows)
    tile_count = (length + tile_len - 1) // tile_len

    def cache_step(index, state_in):
        old_max, old_total, old_accum = state_in
        first_pos = index * tile_len
        key_tile = lax.dynamic_slice_in_dim(keys_cache, first_pos, tile_len, 0).reshape(
            tile_len, local_heads, head_size
        )
        value_tile = lax.dynamic_slice_in_dim(values_cache, first_pos, tile_len, 0).reshape(
            tile_len, local_heads, head_size
        )
        key_pos = first_pos + jnp.arange(tile_len)
        tile_scores = (
            jnp.einsum("qhd,khd->hqk", queries, key_tile, preferred_element_type=jnp.float32)
            * score_scale
        )
        gaps = (query_pos[:, None] - key_pos[None, :]).astype(jnp.float32)
        tile_scores = tile_scores - slopes[:, None, None] * gaps[None, :, :]
        tile_scores = jnp.where((key_pos < length)[None, None, :], tile_scores, -jnp.inf)
        new_max = jnp.maximum(old_max, jnp.max(tile_scores, axis=-1))
        shrink = jnp.exp(old_max - new_max)
        tile_weights = jnp.exp(tile_scores - new_max[..., None])
        new_total = old_total * shrink + jnp.sum(tile_weights, axis=-1)
        new_accum = old_accum * shrink[..., None] + jnp.einsum(
            "hqk,khd->hqd",
            tile_weights.astype(jnp.bfloat16),
            value_tile,
            preferred_element_type=jnp.float32,
        )
        return (new_max, new_total, new_accum)

    row_max, row_total, accum = lax.fori_loop(
        0, tile_count, cache_step, (row_max, row_total, accum)
    )
    context = (accum / row_total[..., None]).astype(jnp.bfloat16)
    return jnp.transpose(context, (1, 0, 2)).reshape(block_len, local_heads * head_size)


def shards(
    embeds,
    input_norm_gain,
    input_norm_bias,
    joined_projection_weight,
    joined_projection_bias,
    adapter_down_weight,
    adapter_up_weight,
    attention_out_weight,
    attention_out_bias,
    post_attention_norm_gain,
    post_attention_norm_bias,
    feedforward_up_weight,
    feedforward_up_bias,
    feedforward_down_weight,
    feedforward_down_bias,
    stored_keys,
    stored_values,
    stored_length,
    tenant_first_request,
    accept,
    replacement_token_index,
    word_embedding_table,
):
    tp_rank = lax.axis_index("tp")
    req_rank = lax.axis_index("req")
    local_heads = joined_projection_weight.shape[1] // (3 * HD)
    requests = stored_keys.shape[0]
    tok_rows = requests * BLK
    share_rows = embeds.shape[0]
    table_rows = word_embedding_table.shape[0]
    head_index = tp_rank * local_heads + jnp.arange(local_heads)
    slopes = jnp.exp2(-8.0 * (head_index + 1).astype(jnp.float32) / H)
    owned = req_rank * requests + jnp.arange(requests)
    tenant_index = jnp.sum(
        (owned[:, None] >= tenant_first_request[None, :]).astype(jnp.int32), axis=1
    )
    adapter_inputs = [
        lax.dynamic_index_in_dim(adapter_down_weight, tenant_index[0], 0, keepdims=False)
    ]
    adapter_outputs = [
        lax.dynamic_index_in_dim(adapter_up_weight, tenant_index[0], 0, keepdims=False)
    ]

    def project(shard_rows):
        joined = jnp.dot(shard_rows, joined_projection_weight, preferred_element_type=jnp.float32)
        row_request = jnp.arange(shard_rows.shape[0]) // BLK
        low_rank_rows = jnp.dot(
            shard_rows, adapter_inputs[0], preferred_element_type=jnp.float32
        ).astype(jnp.bfloat16)
        lifted = jnp.dot(low_rank_rows, adapter_outputs[0], preferred_element_type=jnp.float32)
        joined = joined + jnp.where((row_request == 0)[:, None], lifted, 0.0)
        return (joined + joined_projection_bias).astype(jnp.bfloat16)

    def expand(shard_rows):
        inner = (
            jnp.dot(shard_rows, feedforward_up_weight, preferred_element_type=jnp.float32)
            + feedforward_up_bias
        )
        return jax.nn.gelu(inner, approximate=True).astype(jnp.bfloat16)

    def share_sum(left, right):
        partial_sum = jnp.dot(left, right, preferred_element_type=jnp.float32)
        summed = lax.psum(partial_sum.astype(jnp.bfloat16), "tp").astype(jnp.float32)
        return lax.dynamic_slice_in_dim(summed, tp_rank * share_rows, share_rows, 0)

    def run_layer_pass(residual_state):
        normed = layer_norm(residual_state, input_norm_gain, input_norm_bias)
        joined = project(lax.all_gather(normed, "tp", axis=0, tiled=True))
        heads_view = joined.reshape(tok_rows, local_heads, 3, HD)
        contexts = attend(
            heads_view[:, :, 0],
            heads_view[:, :, 1],
            heads_view[:, :, 2],
            stored_keys[0],
            stored_values[0],
            stored_length[0],
            slopes,
        )
        attended = (
            residual_state.astype(jnp.float32)
            + share_sum(contexts, attention_out_weight)
            + attention_out_bias
        ).astype(jnp.bfloat16)
        post = layer_norm(attended, post_attention_norm_gain, post_attention_norm_bias)
        hidden = expand(lax.all_gather(post, "tp", axis=0, tiled=True))
        return (
            attended.astype(jnp.float32)
            + share_sum(hidden, feedforward_down_weight)
            + feedforward_down_bias
        ).astype(jnp.bfloat16)

    all_ids = lax.all_gather(replacement_token_index, "req", axis=0, tiled=True)
    local_index = all_ids - req_rank * table_rows
    inside = (local_index >= 0) & (local_index < table_rows)
    found = jnp.take(word_embedding_table, jnp.clip(local_index, 0, table_rows - 1), axis=0)
    columns = lax.psum_scatter(
        jnp.where(inside[:, None], found.astype(jnp.float32), 0.0).astype(jnp.bfloat16),
        "req",
        scatter_dimension=0,
        tiled=True,
    )
    replacement = lax.all_to_all(columns, "tp", split_axis=0, concat_axis=1, tiled=True)
    first = run_layer_pass(embeds)
    second_in = jnp.where((accept == 1)[:, None], replacement, first)
    return run_layer_pass(second_in)


def solution(mesh):
    in_specs = (
        P(("req", "tp"), None),
        P(),
        P(),
        P(None, "tp"),
        P("tp"),
        P(),
        P(None, None, "tp"),
        P("tp", None),
        P(),
        P(),
        P(),
        P(None, "tp"),
        P("tp"),
        P("tp", None),
        P(),
        P("req", None, "tp"),
        P("req", None, "tp"),
        P("req"),
        P(),
        P(("req", "tp")),
        P("req"),
        P("req", "tp"),
    )
    out_specs = P(("req", "tp"), None)
    return jax.shard_map(shards, mesh=mesh, in_specs=in_specs, out_specs=out_specs, check_vma=False)
```

profile of v0, /device:TPU:0, one launch (start us, length us, event | category | flops | bytes accessed | tf_op | source)
XLA Modules:
  0.0 432.1 jit_solution(809088786829762818)
XLA Ops:
  16.5 2.3 copy.68
  19.5 23.0 %all-gather.6.cloned.1.call-done = bf16[256,2048]{1,0:T(8,128)(2,1)} async-done(((bf16[64,2048]{1,0:T(8,128)(2,1)}), bf16[256,2048]{1,0:T(8,128)(2,1)}) %all-gather.6.cloned.1.call-update) | async-done | bytes 1048592 | tf_op jit(solution)/shard_map/all_gather | solution.py:150
  42.5 6.1 %fusion.131 = f32[256,1536]{1,0:T(8,128)} fusion(bf16[256,2048]{1,0:T(8,128)(2,1)} %all-gather.6.cloned.1.call-done, bf16[2048,1536]{1,0:T(8,128)(2,1)} %param.29), kind=kOutput, calls=%fused_computation.196 | convolution fusion | flops 1610612736 | bytes 8912896 | tf_op jit(solution)/shard_map/dot_general | solution.py:127
  48.6 3.8 fusion.23
  52.4 2.3 copy.62
  60.2 5.2 %while.32 = (s32[]{:T(128)}, f32[4,256]{1,0:T(4,128)S(1)}, f32[4,256]{1,0:T(4,128)S(1)}, f32[4,256,128]{2,1,0:T(8,128)}, s32[]{:T(128)}, /*index=5*/s32[]{:T(128...) while((s32[]{:T(128)}, f32[4,256]{1,0:T(4,128)S(1)}, ...), condition=%wide.region_9.10_spmd.clone.clone, body=%wide.region_6.9_spmd.clone.clone.sunk | while | flops 273682176 | bytes 17112384 | solution.py:75
  70.4 55.7 %all-reduce.5.cloned.1.call-done = bf16[256,2048]{1,0:T(8,128)(2,1)} async-done(((bf16[256,2048]{1,0:T(8,128)(2,1)}), bf16[256,2048]{1,0:T(8,128)(2,1)}) %all-reduce.5.cloned.1.call-update) | async-done | bytes 1048592 | tf_op jit(solution)/shard_map/psum | solution.py:145
  128.9 8.9 %all-gather = s32[8,1,256]{2,1,0:T(1,128)S(1)} all-gather(s32[1,1,256]{2,1,0:T(1,128)S(1)} %bitcast.137), channel_id=1, replica_groups=mesh['req'=8,'tp'=4] {'req'}, dimensions={0}, use_global_device_ids=true | all-gather | bytes 9216 | tf_op jit(solution)/shard_map/all_gather | solution.py:174
  137.8 12.9 %gather_fusion = bf16[2048,512]{1,0:T(8,128)(2,1)} fusion(bf16[6272,512]{1,0:T(8,128)(2,1)} %param.47, s32[2048]{0:T(1024)S(1)} %fusion.107), kind=kCustom, calls=%fused_computation | custom fusion | bytes 4202496 | tf_op jit(solution)/shard_map/jit(_take)/gather | solution.py:177
  150.7 3.0 select_convert_fusion
  153.8 2.5 all-gather.8.cloned.1.call-done
  156.3 7.7 %convolution_convert_fusion.3 = bf16[256,2048]{1,0:T(8,128)(2,1)} fusion(bf16[1024,2048]{1,0:T(8,128)(2,1)} %param.39, bf16[256,2048]{1,0:T(8,128)(2,1)} %all-gather.8.cloned.1.call-done, bf16[2048,1024]{1,0:T(8,128)(2,1)} %param.37, f32[1024]{0:T(1024)S(1)} %copy-done.18), kind=kOutput, calls=%fused_computation.49 | convolution fusion | flops 2150629376 | bytes 10489856 | tf_op jit(solution)/shard_map/dot_general | solution.py:144
  164.0 29.5 %reduce-scatter.2.cloned.1.call-done = bf16[256,512]{1,0:T(8,128)(2,1)} async-done(((bf16[2048,512]{1,0:T(8,128)(2,1)}), bf16[256,512]{1,0:T(8,128)(2,1)}) %reduce-scatter.2.cloned.1.call-update) | async-done | bytes 262160 | tf_op jit(solution)/shard_map/reduce_scatter | solution.py:178
  193.5 4.6 %all-to-all-start = ((bf16[4,64,512]{2,1,0:T(8,128)(2,1)}), bf16[4,64,512]{2,1,0:T(8,128)(2,1)S(1)}, u32[]{:S(2)}, u32[]{:S(2)}) async-start(bf16[4,64,512]{2,1,0:T(8,128)(2,1)} %bitcast.134), calls=%async_computation.1 | async-start | bytes 524288 | tf_op jit(solution)/shard_map/all_to_all | solution.py:184
  198.1 16.4 %all-to-all-done = bf16[4,64,512]{2,1,0:T(8,128)(2,1)S(1)} async-done(((bf16[4,64,512]{2,1,0:T(8,128)(2,1)}), bf16[4,64,512]{2,1,0:T(8,128)(2,1)S(1)}, u32[]{:S(2)}, u32[]{:S(2)}) %all-to-all-start) | async-done | bytes 262176 | tf_op jit(solution)/shard_map/all_to_all | solution.py:184
  215.2 6.2 %all-reduce.7.cloned.1.call-done = bf16[256,2048]{1,0:T(8,128)(2,1)} async-done(((bf16[256,2048]{1,0:T(8,128)(2,1)}), bf16[256,2048]{1,0:T(8,128)(2,1)}) %all-reduce.7.cloned.1.call-update) | async-done | bytes 1048592 | tf_op jit(solution)/shard_map/psum | solution.py:145
  224.0 26.8 %all-gather.10.cloned.1.call-done = bf16[256,2048]{1,0:T(8,128)(2,1)} async-done(((bf16[64,2048]{1,0:T(8,128)(2,1)}), bf16[256,2048]{1,0:T(8,128)(2,1)}) %all-gather.10.cloned.1.call-update) | async-done | bytes 1048592 | tf_op jit(solution)/shard_map/all_gather | solution.py:150
  250.9 6.1 %fusion.132 = f32[256,1536]{1,0:T(8,128)} fusion(bf16[256,2048]{1,0:T(8,128)(2,1)} %all-gather.10.cloned.1.call-done, bf16[2048,1536]{1,0:T(8,128)(2,1)} %param.29), kind=kOutput, calls=%fused_computation.197 | convolution fusion | flops 1610612736 | bytes 8912896 | tf_op jit(solution)/shard_map/dot_general | solution.py:127
  256.9 3.8 fusion.22
  270.3 5.2 %while.33 = (s32[]{:T(128)}, f32[4,256]{1,0:T(4,128)S(1)}, f32[4,256]{1,0:T(4,128)S(1)}, f32[4,256,128]{2,1,0:T(8,128)}, s32[]{:T(128)}, /*index=5*/s32[]{:T(128...) while((s32[]{:T(128)}, f32[4,256]{1,0:T(4,128)S(1)}, ...), condition=%wide.region_21.22_spmd.clone.clone, body=%wide.region_18.21_spmd.clone.clone.sunk | while | flops 273682176 | bytes 17112384 | solution.py:75
  278.6 55.7 %all-reduce.9.cloned.1.call-done = bf16[256,2048]{1,0:T(8,128)(2,1)} async-done(((bf16[256,2048]{1,0:T(8,128)(2,1)}), bf16[256,2048]{1,0:T(8,128)(2,1)}) %all-reduce.9.cloned.1.call-update) | async-done | bytes 1048592 | tf_op jit(solution)/shard_map/psum | solution.py:145
  336.6 27.4 %all-gather.12.cloned.1.call-done = bf16[256,2048]{1,0:T(8,128)(2,1)} async-done(((bf16[64,2048]{1,0:T(8,128)(2,1)}), bf16[256,2048]{1,0:T(8,128)(2,1)}) %all-gather.12.cloned.1.call-update) | async-done | bytes 1048592 | tf_op jit(solution)/shard_map/all_gather | solution.py:167
  364.0 7.4 %convolution_convert_fusion.2 = bf16[256,2048]{1,0:T(8,128)(2,1)} fusion(bf16[1024,2048]{1,0:T(8,128)(2,1)} %param.39, bf16[256,2048]{1,0:T(8,128)(2,1)} %all-gather.12.cloned.1.call-done, bf16[2048,1024]{1,0:T(8,128)(2,1)} %param.37, f32[1024]{0:T(1024)S(1)} %copy-done.18), kind=kOutput, calls=%fused_computation.48 | convolution fusion | flops 2150629376 | bytes 10489856 | tf_op jit(solution)/shard_map/dot_general | solution.py:144
  371.4 51.5 %all-reduce.11.cloned.1.call-done = bf16[256,2048]{1,0:T(8,128)(2,1)} async-done(((bf16[256,2048]{1,0:T(8,128)(2,1)}), bf16[256,2048]{1,0:T(8,128)(2,1)}) %all-reduce.11.cloned.1.call-update) | async-done | bytes 1048592 | tf_op jit(solution)/shard_map/psum | solution.py:145
  (132 shorter events, 50.7 us)
Async XLA Ops:
  7.4 61.1 %copy-start = (bf16[512,2048]{1,0:T(8,128)(2,1)S(1)}, bf16[512,2048]{1,0:T(8,128)(2,1)}, u32[]{:S(2)}) copy-start(bf16[512,2048]{1,0:T(8,128)(2,1)} %param.33) | copy-start | bytes 6291460
  7.4 35.1 %all-gather.6.cloned.1.call-start = ((), (), s32[]{:S(2)}) async-start(), calls=%async_computation.3 | async-start | bytes 1310720 | tf_op jit(solution)/shard_map/all_gather | solution.py:150
  11.7 114.4 %all-reduce.5.cloned.1.call-start = ((), (), s32[]{:S(2)}) async-start(), calls=%async_computation.4 | async-start | bytes 2097152 | tf_op jit(solution)/shard_map/psum | solution.py:145
  19.5 35.2 %copy-start.7 = (f32[256,256]{0,1:T(8,128)}, f32[256,256]{0,1:T(8,128)S(1)}, u32[]{:S(2)}) copy-start(f32[256,256]{0,1:T(8,128)S(1)} %abs_convert_fusion) | copy-start | bytes 786436
  19.5 29.0 %copy-start.12 = (f32[1536]{0:T(1024)S(1)}, f32[1536]{0:T(1024)}, u32[]{:S(2)}) copy-start(f32[1536]{0:T(1024)} %param.30) | copy-start | bytes 18436
  60.2 2.7 copy-start.9
  68.5 57.6 %copy-start.6 = (bf16[64,2048]{1,0:T(8,128)(2,1)S(1)}, bf16[64,2048]{1,0:T(8,128)(2,1)}, u32[]{:S(2)}) copy-start(bf16[64,2048]{1,0:T(8,128)(2,1)} %param.26) | copy-start | bytes 786436
  68.5 57.6 %copy-start.13 = (f32[2048]{0:T(1024)S(1)}, f32[2048]{0:T(1024)}, u32[]{:S(2)}) copy-start(f32[2048]{0:T(1024)} %param.34) | copy-start | bytes 24580
  68.5 59.4 %copy-start.14 = (f32[2048]{0:T(1024)S(1)}, f32[2048]{0:T(1024)}, u32[]{:S(2)}) copy-start(f32[2048]{0:T(1024)} %param.36) | copy-start | bytes 24580
  68.5 59.4 %copy-start.15 = (f32[2048]{0:T(1024)S(1)}, f32[2048]{0:T(1024)}, u32[]{:S(2)}) copy-start(f32[2048]{0:T(1024)} %param.35) | copy-start | bytes 24580
  70.3 58.6 %copy-start.17 = (s32[256]{0:T(256)S(1)}, s32[256]{0:T(256)}, u32[]{:S(2)}) copy-start(s32[256]{0:T(256)} %param.46) | copy-start | bytes 3076
  70.3 86.0 %all-gather.8.cloned.1.call-start = ((), (), s32[]{:S(2)}) async-start(), calls=%async_computation.5 | async-start | bytes 1310720 | tf_op jit(solution)/shard_map/all_gather | solution.py:167
  128.8 64.7 %reduce-scatter.2.cloned.1.call-start = ((), (), s32[]{:S(2)}) async-start(), calls=%async_computation.2 | async-start | bytes 2359296 | tf_op jit(solution)/shard_map/reduce_scatter | solution.py:178
  153.7 44.4 %copy-start.19 = (s32[64]{0:T(128)S(1)}, s32[64]{0:T(128)}, u32[]{:S(2)}) copy-start(s32[64]{0:T(128)} %param.45) | copy-start | bytes 772
  153.7 67.7 %all-reduce.7.cloned.1.call-start = ((), (), s32[]{:S(2)}) async-start(), calls=%async_computation.6 | async-start | bytes 2097152 | tf_op jit(solution)/shard_map/psum | solution.py:145
  164.0 57.5 %copy-start.16 = (f32[2048]{0:T(1024)S(1)}, f32[2048]{0:T(1024)}, u32[]{:S(2)}) copy-start(f32[2048]{0:T(1024)} %param.40) | copy-start | bytes 24580
  164.0 59.1 %copy-start.10 = (f32[2048]{0:T(1024)S(1)}, f32[2048]{0:T(1024)}, u32[]{:S(2)}) copy-start(f32[2048]{0:T(1024)} %param.28) | copy-start | bytes 24580
  164.0 59.1 %copy-start.11 = (f32[2048]{0:T(1024)S(1)}, f32[2048]{0:T(1024)}, u32[]{:S(2)}) copy-start(f32[2048]{0:T(1024)} %param.27) | copy-start | bytes 24580
  193.5 21.0 %all-to-all-start = ((bf16[4,64,512]{2,1,0:T(8,128)(2,1)}), bf16[4,64,512]{2,1,0:T(8,128)(2,1)S(1)}, u32[]{:S(2)}, u32[]{:S(2)}) async-start(bf16[4,64,512]{2,1,0:T(8,128)(2,1)} %bitcast.134), calls=%async_computation.1 | async-start | bytes 524288 | tf_op jit(solution)/shard_map/all_to_all | solution.py:184
  198.1 52.8 %all-gather.10.cloned.1.call-start = ((), (), s32[]{:S(2)}) async-start(), calls=%async_computation.7 | async-start | bytes 1310720 | tf_op jit(solution)/shard_map/all_gather | solution.py:150
  224.0 110.3 %all-reduce.9.cloned.1.call-start = ((), (), s32[]{:S(2)}) async-start(), calls=%async_computation.8 | async-start | bytes 2097152 | tf_op jit(solution)/shard_map/psum | solution.py:145
  270.3 2.7 copy-start.8
  278.5 85.5 %all-gather.12.cloned.1.call-start = ((), (), s32[]{:S(2)}) async-start(), calls=%async_computation.9 | async-start | bytes 1310720 | tf_op jit(solution)/shard_map/all_gather | solution.py:167
  336.6 86.3 %all-reduce.11.cloned.1.call-start = ((), (), s32[]{:S(2)}) async-start(), calls=%async_computation.10 | async-start | bytes 2097152 | tf_op jit(solution)/shard_map/psum | solution.py:145
  (6 other events, 7.0 us)
Sparse Core Ops, SparseCore 0:
  11.8 30.6 all-gather.5
  70.4 55.5 all-reduce.4
  128.9 27.3 all-gather.7
  164.1 57.2 all-reduce.6
  224.1 26.7 all-gather.9
  278.6 55.5 all-reduce.8
  336.7 27.3 all-gather.11
  371.5 51.3 all-reduce.10
Sparse Core Ops, SparseCore 1:
  153.8 39.7 reduce-scatter.1
where the time goes:
time: 433 us; the launch traced here: 432 us
  waiting for transfers between devices  295 us (68%)
  matrix products  48.1 us (11%)
  local copies, waits for them, and re-layouts  35 us (8%)
  other arithmetic  22.4 us (5%)
  between operations  17.8 us (4%)
  blocking collectives  8.86 us (2%)
  starting transfers between devices  4.9 us (1%)
    psum x4, waiting for transfers between devices, share_sum(): lax.psum(partial_sum.astype(jnp.bfloat16), 'tp').astype(jnp.float32)  169 us
    all_gather x2, waiting for transfers between devices, run_layer_pass(): joined = project(lax.all_gather(normed, 'tp', axis=0, tiled=True))  49.8 us
    all_gather x2, waiting for transfers between devices, run_layer_pass(): hidden = expand(lax.all_gather(post, 'tp', axis=0, tiled=True))  29.9 us
    reduce_scatter x1, waiting for transfers between devices, shards(): lax.psum_scatter(jnp.where(inside[:, None], found.astype(jnp.float32), 0....  29.5 us
    dot_general x4, matrix products, share_sum(): partial_sum = jnp.dot(left, right, preferred_element_type=jnp.float32)  18.6 us
    all_to_all x1, waiting for transfers between devices, shards(): lax.all_to_all(columns, 'tp', split_axis=0, concat_axis=1, tiled=True)  16.4 us
    gather x1, local copies, waits for them, and re-layouts, shards(): jnp.take(word_embedding_table, jnp.clip(local_index, 0, table_rows - 1),...  12.9 us
    dot_general x2, matrix products, project(): jnp.dot(shard_rows, joined_projection_weight, preferred_element_type=jnp....  12.1 us
  transfers between devices with their start and end apart: 10, of which 10 were waited for; matrix products, arithmetic and copies ran while one was open for 7% of the time, Pallas kernels for 0%

commit v1 on v0

--- a/solution.py
+++ b/solution.py
@@ -7,6 +7,18 @@
 HD = 128
 BLK = 256
 EPSILON = 1e-05
+
+
+def gather_by_bits(array, axis, dim):
+    ways, here, lap = (lax.axis_size(axis), lax.axis_index(axis), array.shape[dim])
+    line, have = (array, 1)
+    while have < ways:
+        line = jnp.concatenate(
+            [line, lax.ppermute(line, axis, [(d, (d - have) % ways) for d in range(ways)])],
+            axis=dim,
+        )
+        have = 2 * have
+    return jnp.roll(line, here * lap, axis=dim)
 
 
 def layer_norm(residual_state, gain, shift):
@@ -147,7 +159,7 @@
 
     def run_layer_pass(residual_state):
         normed = layer_norm(residual_state, input_norm_gain, input_norm_bias)
-        joined = project(lax.all_gather(normed, "tp", axis=0, tiled=True))
+        joined = project(gather_by_bits(normed, "tp", 0))
         heads_view = joined.reshape(tok_rows, local_heads, 3, HD)
         contexts = attend(
             heads_view[:, :, 0],

time: 433 us -> 453 us (1.046)
  other arithmetic: 22.4 us -> 30.7 us
  starting transfers between devices: 4.9 us -> 12.6 us
    ppermute x0 -> x4, waiting for transfers between devices: none -> 54.3 us  [gather_by_bits(): lax.ppermute(line, axis, [(d, (d - have) % ways) for d in range(ways)])]
    all_gather x2 -> x0, waiting for transfers between devices: 49.8 us -> none  [run_layer_pass(): joined = project(lax.all_gather(normed, 'tp', axis=0, tiled=True))]
    concatenate x0 -> x4, other arithmetic: none -> 9.64 us  [the longest x2 7.82 us: gather_by_bits(): return jnp.roll(line, here * lap, axis=dim)]
    ppermute x0 -> x4, starting transfers between devices: none -> 7.61 us  [gather_by_bits(): lax.ppermute(line, axis, [(d, (d - have) % ways) for d in range(ways)])]
  transfers between devices with their start and end apart: 10 -> 12, of which waited for: 10 -> 12; matrix products, arithmetic and copies ran while one was open for 7% -> 7% of each run, Pallas kernels for 0% -> 0%
where the time goes in v1:
time: 453 us; the launch traced here: 452 us
  waiting for transfers between devices  299 us (66%)
  matrix products  47.9 us (11%)
  local copies, waits for them, and re-layouts  35 us (8%)
  other arithmetic  30.7 us (7%)
  between operations  17.8 us (4%)
  starting transfers between devices  12.6 us (3%)
  blocking collectives  8.86 us (2%)
    psum x4, waiting for transfers between devices, share_sum(): lax.psum(partial_sum.astype(jnp.bfloat16), 'tp').astype(jnp.float32)  169 us
    ppermute x4, waiting for transfers between devices, gather_by_bits(): lax.ppermute(line, axis, [(d, (d - have) % ways) for d in range(ways)])  54.3 us
    all_gather x2, waiting for transfers between devices, run_layer_pass(): hidden = expand(lax.all_gather(post, 'tp', axis=0, tiled=True))  29.8 us
    reduce_scatter x1, waiting for transfers between devices, shards(): lax.psum_scatter(jnp.where(inside[:, None], found.astype(jnp.float32), 0....  29.5 us
    dot_general x4, matrix products, share_sum(): partial_sum = jnp.dot(left, right, preferred_element_type=jnp.float32)  18.6 us
    all_to_all x1, waiting for transfers between devices, shards(): lax.all_to_all(columns, 'tp', split_axis=0, concat_axis=1, tiled=True)  16.4 us
    gather x1, local copies, waits for them, and re-layouts, shards(): jnp.take(word_embedding_table, jnp.clip(local_index, 0, table_rows - 1),...  12.9 us
    dot_general x2, matrix products, project(): jnp.dot(shard_rows, joined_projection_weight, preferred_element_type=jnp....  12.4 us
  transfers between devices with their start and end apart: 12, of which 12 were waited for; matrix products, arithmetic and copies ran while one was open for 7% of the time, Pallas kernels for 0%

profile of v1, /device:TPU:0, one launch (start us, length us, event | category | flops | bytes accessed | tf_op | source)
XLA Modules:
  0.0 451.9 jit_solution(7376070617131104787)
XLA Ops:
  11.0 5.1 %collective-permute-start = (bf16[64,2048]{1,0:T(8,128)(2,1)S(1)}, bf16[64,2048]{1,0:T(8,128)(2,1)S(1)}, u32[]{:S(2)}, u32[]{:S(2)}) collective-permute-start(bf16[64,2048]{1,0:T(8,128)(2,1)S(1)} %fusion.75), channel_id=1, source_target_pairs={{0,3},{1,0},{2,1},{3,2},{4,7},{5,4},{6,5},{7,6},{8,11},{9,8},{10,9... | collective-permute-start | bytes 786440 | tf_op jit(solution)/shard_map/ppermute | solution.py:17
  16.1 5.6 %collective-permute-done = bf16[64,2048]{1,0:T(8,128)(2,1)S(1)} collective-permute-done((bf16[64,2048]{1,0:T(8,128)(2,1)S(1)}, bf16[64,2048]{1,0:T(8,128)(2,1)S(1)}, u32[]{:S(2)}, u32[]{:S(2)}) %collective-permute-start) | collective-permute-done | bytes 262176 | tf_op jit(solution)/shard_map/ppermute | solution.py:17
  31.9 15.9 %collective-permute-done.1 = bf16[128,2048]{1,0:T(8,128)(2,1)} collective-permute-done((bf16[128,2048]{1,0:T(8,128)(2,1)}, bf16[128,2048]{1,0:T(8,128)(2,1)}, u32[]{:S(2)}, u32[]{:S(2)}) %collective-permute-start.1) | collective-permute-done | bytes 524320 | tf_op jit(solution)/shard_map/ppermute | solution.py:17
  47.8 3.9 fusion.45
  51.7 3.6 convolution_select_fusion.1
  55.3 6.2 %fusion.20 = bf16[256,1536]{1,0:T(8,128)(2,1)} fusion(f32[256,1536]{1,0:T(8,128)} %convolution_select_fusion.1, bf16[256,2048]{1,0:T(8,128)(2,1)} %fusion.45, bf16[2048,1536]{1,0:T(8,128)(2,1)} %param.31, f32[1536]{0:T(1024)S(1)} %copy-done.20), kind=kOutput, calls=%fused_computation.48 | convolution fusion | flops 1611792384 | bytes 9705472 | tf_op jit(solution)/shard_map/dot_general | solution.py:139
  69.3 5.2 %while.32 = (s32[]{:T(128)}, f32[4,256]{1,0:T(4,128)S(1)}, f32[4,256]{1,0:T(4,128)S(1)}, f32[4,256,128]{2,1,0:T(8,128)}, s32[]{:T(128)}, /*index=5*/s32[]{:T(128...) while((s32[]{:T(128)}, f32[4,256]{1,0:T(4,128)S(1)}, ...), condition=%wide.region_9.11_spmd.clone.clone, body=%wide.region_6.10_spmd.clone.clone.sunk | while | flops 273682176 | bytes 17112384 | solution.py:87
  79.5 56.2 %all-reduce.5.cloned.1.call-done = bf16[256,2048]{1,0:T(8,128)(2,1)} async-done(((bf16[256,2048]{1,0:T(8,128)(2,1)}), bf16[256,2048]{1,0:T(8,128)(2,1)}) %all-reduce.5.cloned.1.call-update) | async-done | bytes 1048592 | tf_op jit(solution)/shard_map/psum | solution.py:157
  138.5 8.9 %all-gather = s32[8,1,256]{2,1,0:T(1,128)S(1)} all-gather(s32[1,1,256]{2,1,0:T(1,128)S(1)} %bitcast.137), channel_id=1, replica_groups=mesh['req'=8,'tp'=4] {'req'}, dimensions={0}, use_global_device_ids=true | all-gather | bytes 9216 | tf_op jit(solution)/shard_map/all_gather | solution.py:186
  147.5 12.9 %gather_fusion = bf16[2048,512]{1,0:T(8,128)(2,1)} fusion(bf16[6272,512]{1,0:T(8,128)(2,1)} %param.49, s32[2048]{0:T(1024)S(1)} %fusion.115), kind=kCustom, calls=%fused_computation | custom fusion | bytes 4202496 | tf_op jit(solution)/shard_map/jit(_take)/gather | solution.py:189
  165.9 7.7 %convolution_convert_fusion.3 = bf16[256,2048]{1,0:T(8,128)(2,1)} fusion(bf16[1024,2048]{1,0:T(8,128)(2,1)} %param.41, bf16[256,2048]{1,0:T(8,128)(2,1)} %all-gather.4.cloned.1.call-done, bf16[2048,1024]{1,0:T(8,128)(2,1)} %param.39, f32[1024]{0:T(1024)S(1)} %copy-done.21), kind=kOutput, calls=%fused_computation.47 | convolution fusion | flops 2150629376 | bytes 10489856 | tf_op jit(solution)/shard_map/dot_general | solution.py:156
  173.6 29.5 %reduce-scatter.2.cloned.1.call-done = bf16[256,512]{1,0:T(8,128)(2,1)} async-done(((bf16[2048,512]{1,0:T(8,128)(2,1)}), bf16[256,512]{1,0:T(8,128)(2,1)}) %reduce-scatter.2.cloned.1.call-update) | async-done | bytes 262160 | tf_op jit(solution)/shard_map/reduce_scatter | solution.py:190
  203.1 4.6 %all-to-all-start = ((bf16[4,64,512]{2,1,0:T(8,128)(2,1)}), bf16[4,64,512]{2,1,0:T(8,128)(2,1)S(1)}, u32[]{:S(2)}, u32[]{:S(2)}) async-start(bf16[4,64,512]{2,1,0:T(8,128)(2,1)} %bitcast.134), calls=%async_computation.1 | async-start | bytes 524288 | tf_op jit(solution)/shard_map/all_to_all | solution.py:196
  207.8 16.4 %all-to-all-done = bf16[4,64,512]{2,1,0:T(8,128)(2,1)S(1)} async-done(((bf16[4,64,512]{2,1,0:T(8,128)(2,1)}), bf16[4,64,512]{2,1,0:T(8,128)(2,1)S(1)}, u32[]{:S(2)}, u32[]{:S(2)}) %all-to-all-start) | async-done | bytes 262176 | tf_op jit(solution)/shard_map/all_to_all | solution.py:196
  224.9 6.2 %all-reduce.7.cloned.1.call-done = bf16[256,2048]{1,0:T(8,128)(2,1)} async-done(((bf16[256,2048]{1,0:T(8,128)(2,1)}), bf16[256,2048]{1,0:T(8,128)(2,1)}) %all-reduce.7.cloned.1.call-update) | async-done | bytes 1048592 | tf_op jit(solution)/shard_map/psum | solution.py:157
  234.0 7.3 %collective-permute-done.2 = bf16[64,2048]{1,0:T(8,128)(2,1)S(1)} collective-permute-done((bf16[64,2048]{1,0:T(8,128)(2,1)S(1)}, bf16[64,2048]{1,0:T(8,128)(2,1)S(1)}, u32[]{:S(2)}, u32[]{:S(2)}) %collective-permute-start.2) | collective-permute-done | bytes 262176 | tf_op jit(solution)/shard_map/ppermute | solution.py:17
  242.2 25.5 %collective-permute-done.3 = bf16[128,2048]{1,0:T(8,128)(2,1)} collective-permute-done((bf16[128,2048]{1,0:T(8,128)(2,1)}, bf16[128,2048]{1,0:T(8,128)(2,1)}, u32[]{:S(2)}, u32[]{:S(2)}) %collective-permute-start.3) | collective-permute-done | bytes 524320 | tf_op jit(solution)/shard_map/ppermute | solution.py:17
  267.7 3.9 fusion.40
  275.2 6.2 %fusion.21 = bf16[256,1536]{1,0:T(8,128)(2,1)} fusion(f32[256,1536]{1,0:T(8,128)} %convolution_select_fusion, bf16[256,2048]{1,0:T(8,128)(2,1)} %fusion.40, bf16[2048,1536]{1,0:T(8,128)(2,1)} %param.31, f32[1536]{0:T(1024)S(1)} %copy-done.20), kind=kOutput, calls=%fused_computation.49 | convolution fusion | flops 1611792384 | bytes 9705472 | tf_op jit(solution)/shard_map/dot_general | solution.py:139
  290.8 5.2 %while.33 = (s32[]{:T(128)}, f32[4,256]{1,0:T(4,128)S(1)}, f32[4,256]{1,0:T(4,128)S(1)}, f32[4,256,128]{2,1,0:T(8,128)}, s32[]{:T(128)}, /*index=5*/s32[]{:T(128...) while((s32[]{:T(128)}, f32[4,256]{1,0:T(4,128)S(1)}, ...), condition=%wide.region_21.23_spmd.clone.clone, body=%wide.region_18.22_spmd.clone.clone.sunk | while | flops 273682176 | bytes 17112384 | solution.py:87
  299.1 55.0 %all-reduce.9.cloned.1.call-done = bf16[256,2048]{1,0:T(8,128)(2,1)} async-done(((bf16[256,2048]{1,0:T(8,128)(2,1)}), bf16[256,2048]{1,0:T(8,128)(2,1)}) %all-reduce.9.cloned.1.call-update) | async-done | bytes 1048592 | tf_op jit(solution)/shard_map/psum | solution.py:157
  356.5 27.4 %all-gather.6.cloned.1.call-done = bf16[256,2048]{1,0:T(8,128)(2,1)} async-done(((bf16[64,2048]{1,0:T(8,128)(2,1)}), bf16[256,2048]{1,0:T(8,128)(2,1)}) %all-gather.6.cloned.1.call-update) | async-done | bytes 1048592 | tf_op jit(solution)/shard_map/all_gather | solution.py:179
  383.9 7.3 %convolution_convert_fusion.2 = bf16[256,2048]{1,0:T(8,128)(2,1)} fusion(bf16[1024,2048]{1,0:T(8,128)(2,1)} %param.41, bf16[256,2048]{1,0:T(8,128)(2,1)} %all-gather.6.cloned.1.call-done, bf16[2048,1024]{1,0:T(8,128)(2,1)} %param.39, f32[1024]{0:T(1024)S(1)} %copy-done.21), kind=kOutput, calls=%fused_computation.46 | convolution fusion | flops 2150629376 | bytes 10489856 | tf_op jit(solution)/shard_map/dot_general | solution.py:156
  391.3 51.5 %all-reduce.11.cloned.1.call-done = bf16[256,2048]{1,0:T(8,128)(2,1)} async-done(((bf16[256,2048]{1,0:T(8,128)(2,1)}), bf16[256,2048]{1,0:T(8,128)(2,1)}) %all-reduce.11.cloned.1.call-update) | async-done | bytes 1048592 | tf_op jit(solution)/shard_map/psum | solution.py:157
  (146 shorter events, 67.2 us)
Async XLA Ops:
  7.4 70.3 %copy-start = (bf16[512,2048]{1,0:T(8,128)(2,1)S(1)}, bf16[512,2048]{1,0:T(8,128)(2,1)}, u32[]{:S(2)}) copy-start(bf16[512,2048]{1,0:T(8,128)(2,1)} %param.35) | copy-start | bytes 6291460
  7.4 16.7 %copy-start.22 = (s32[3]{0:T(128)S(1)}, s32[3]{0:T(128)}, u32[]{:S(2)}) copy-start(s32[3]{0:T(128)} %param.46) | copy-start | bytes 40
  7.4 128.3 %all-reduce.5.cloned.1.call-start = ((), (), s32[]{:S(2)}) async-start(), calls=%async_computation.3 | async-start | bytes 2097152 | tf_op jit(solution)/shard_map/psum | solution.py:157
  11.0 10.7 %collective-permute-start = (bf16[64,2048]{1,0:T(8,128)(2,1)S(1)}, bf16[64,2048]{1,0:T(8,128)(2,1)S(1)}, u32[]{:S(2)}, u32[]{:S(2)}) collective-permute-start(bf16[64,2048]{1,0:T(8,128)(2,1)S(1)} %fusion.75), channel_id=1, source_target_pairs={{0,3},{1,0},{2,1},{3,2},{4,7},{5,4},{6,5},{7,6},{8,11},{9,8},{10,9... | collective-permute-start | bytes 786440 | tf_op jit(solution)/shard_map/ppermute | solution.py:17
  22.6 25.2 %collective-permute-start.1 = (bf16[128,2048]{1,0:T(8,128)(2,1)}, bf16[128,2048]{1,0:T(8,128)(2,1)}, u32[]{:S(2)}, u32[]{:S(2)}) collective-permute-start(bf16[128,2048]{1,0:T(8,128)(2,1)} %pad_maximum_fusion), channel_id=1, source_target_pairs={{0,2},{1,3},{2,0},{3,1},{4,6},{5,7},{6,4},{7,5},{8,10},{9,11},{10,... | collective-permute-start | bytes 1572872 | tf_op jit(solution)/shard_map/ppermute | solution.py:17
  31.9 23.4 %copy-start.20 = (f32[1536]{0:T(1024)S(1)}, f32[1536]{0:T(1024)}, u32[]{:S(2)}) copy-start(f32[1536]{0:T(1024)} %param.32) | copy-start | bytes 18436
  77.6 58.1 %copy-start.6 = (bf16[64,2048]{1,0:T(8,128)(2,1)S(1)}, bf16[64,2048]{1,0:T(8,128)(2,1)}, u32[]{:S(2)}) copy-start(bf16[64,2048]{1,0:T(8,128)(2,1)} %param.28) | copy-start | bytes 786436
  77.7 58.0 %copy-start.15 = (f32[2048]{0:T(1024)S(1)}, f32[2048]{0:T(1024)}, u32[]{:S(2)}) copy-start(f32[2048]{0:T(1024)} %param.36) | copy-start | bytes 24580
  77.7 59.9 %copy-start.16 = (f32[2048]{0:T(1024)S(1)}, f32[2048]{0:T(1024)}, u32[]{:S(2)}) copy-start(f32[2048]{0:T(1024)} %param.38) | copy-start | bytes 24580
  77.7 59.9 %copy-start.17 = (f32[2048]{0:T(1024)S(1)}, f32[2048]{0:T(1024)}, u32[]{:S(2)}) copy-start(f32[2048]{0:T(1024)} %param.37) | copy-start | bytes 24580
  79.5 59.1 %copy-start.19 = (s32[256]{0:T(256)S(1)}, s32[256]{0:T(256)}, u32[]{:S(2)}) copy-start(s32[256]{0:T(256)} %param.48) | copy-start | bytes 3076
  79.5 86.4 %all-gather.4.cloned.1.call-start = ((), (), s32[]{:S(2)}) async-start(), calls=%async_computation.4 | async-start | bytes 1310720 | tf_op jit(solution)/shard_map/all_gather | solution.py:179
  138.4 64.7 %reduce-scatter.2.cloned.1.call-start = ((), (), s32[]{:S(2)}) async-start(), calls=%async_computation.2 | async-start | bytes 2359296 | tf_op jit(solution)/shard_map/reduce_scatter | solution.py:190
  163.3 44.4 %copy-start.23 = (s32[64]{0:T(128)S(1)}, s32[64]{0:T(128)}, u32[]{:S(2)}) copy-start(s32[64]{0:T(128)} %param.47) | copy-start | bytes 772
  163.3 67.7 %all-reduce.7.cloned.1.call-start = ((), (), s32[]{:S(2)}) async-start(), calls=%async_computation.5 | async-start | bytes 2097152 | tf_op jit(solution)/shard_map/psum | solution.py:157
  173.6 57.5 %copy-start.18 = (f32[2048]{0:T(1024)S(1)}, f32[2048]{0:T(1024)}, u32[]{:S(2)}) copy-start(f32[2048]{0:T(1024)} %param.42) | copy-start | bytes 24580
  173.6 59.1 %copy-start.13 = (f32[2048]{0:T(1024)S(1)}, f32[2048]{0:T(1024)}, u32[]{:S(2)}) copy-start(f32[2048]{0:T(1024)} %param.30) | copy-start | bytes 24580
  173.6 59.1 %copy-start.14 = (f32[2048]{0:T(1024)S(1)}, f32[2048]{0:T(1024)}, u32[]{:S(2)}) copy-start(f32[2048]{0:T(1024)} %param.29) | copy-start | bytes 24580
  203.1 21.0 %all-to-all-start = ((bf16[4,64,512]{2,1,0:T(8,128)(2,1)}), bf16[4,64,512]{2,1,0:T(8,128)(2,1)S(1)}, u32[]{:S(2)}, u32[]{:S(2)}) async-start(bf16[4,64,512]{2,1,0:T(8,128)(2,1)} %bitcast.134), calls=%async_computation.1 | async-start | bytes 524288 | tf_op jit(solution)/shard_map/all_to_all | solution.py:196
  207.7 146.3 %all-reduce.9.cloned.1.call-start = ((), (), s32[]{:S(2)}) async-start(), calls=%async_computation.6 | async-start | bytes 2097152 | tf_op jit(solution)/shard_map/psum | solution.py:157
  232.9 8.3 %collective-permute-start.2 = (bf16[64,2048]{1,0:T(8,128)(2,1)S(1)}, bf16[64,2048]{1,0:T(8,128)(2,1)S(1)}, u32[]{:S(2)}, u32[]{:S(2)}) collective-permute-start(bf16[64,2048]{1,0:T(8,128)(2,1)S(1)} %fusion.67), channel_id=1, source_target_pairs={{0,3},{1,0},{2,1},{3,2},{4,7},{5,4},{6,5},{7,6},{8,11},{9,8},{10,9... | collective-permute-start | bytes 786440 | tf_op jit(solution)/shard_map/ppermute | solution.py:17
  242.2 25.5 %collective-permute-start.3 = (bf16[128,2048]{1,0:T(8,128)(2,1)}, bf16[128,2048]{1,0:T(8,128)(2,1)}, u32[]{:S(2)}, u32[]{:S(2)}) collective-permute-start(bf16[128,2048]{1,0:T(8,128)(2,1)} %pad_maximum_fusion.1), channel_id=1, source_target_pairs={{0,2},{1,3},{2,0},{3,1},{4,6},{5,7},{6,4},{7,5},{8,10},{9,11},{10,... | collective-permute-start | bytes 1572872 | tf_op jit(solution)/shard_map/ppermute | solution.py:17
  299.1 84.8 %all-gather.6.cloned.1.call-start = ((), (), s32[]{:S(2)}) async-start(), calls=%async_computation.7 | async-start | bytes 1310720 | tf_op jit(solution)/shard_map/all_gather | solution.py:179
  356.4 86.3 %all-reduce.11.cloned.1.call-start = ((), (), s32[]{:S(2)}) async-start(), calls=%async_computation.8 | async-start | bytes 2097152 | tf_op jit(solution)/shard_map/psum | solution.py:157
  (12 other events, 35.1 us)
Sparse Core Ops, SparseCore 0:
  79.6 56.0 all-reduce.4
  138.6 27.3 all-gather.3
  173.8 57.2 all-reduce.6
  299.2 54.8 all-reduce.8
  356.5 27.3 all-gather.5
  391.4 51.3 all-reduce.10
Sparse Core Ops, SparseCore 1:
  163.4 39.7 reduce-scatter.1
